TPU v7x, 128 devices: a whole 4x4x4 slice. The times are simulated.
128 devices in a mesh: slab: 8 (over y, z_hi), head: 16 (over x, z_lo, core).
Axes of the slice: x: 4, y: 4, z: 4 (z_hi: 2, z_lo: 2; z = z_hi * 2 + z_lo), core: 2. Of those that a mesh axis runs over, the one named last changes fastest.
Arguments:
- queries: bfloat16 [24576, 4096], P(('slab', 'head')), may hold values from -8 to 8
- keys: bfloat16 [24576, 4096], P(('slab', 'head')), may hold values from -8 to 8
- values: bfloat16 [24576, 4096], P(('slab', 'head')), may hold values from -6 to 6
- neighbours: int32 [64, 12], P('slab'), may hold values from 0 to 63, as said below
- counts: int32 [64], P('slab'), may hold values from 6 to 12
Outputs:
- attended: bfloat16 [24576, 4096], P(('slab', 'head'))
Inputs may be any that keep to these rules, and one draw needn't show every extreme that they name: `neighbours`: for each tile, entries 0 to counts - 1 are distinct tiles whose frame, row and column tile coordinates each differ from the tile's by at most one; entry 0 is the tile itself; the remaining entries equal the tile itself.
All inputs are finite; a program needn't handle non-finite values.
Results may differ from a plain program's by a relative error of at most 0.012.
Values may be sent and summed in bfloat16 or wider, within the bound.
A program may use at most 128 MiB of HBM per device.

v0:
```python
import jax
import jax.numpy as jnp
from jax import lax
from jax.sharding import PartitionSpec as P

HD = 128
TILE = 384


def extended(cells, sides, width):
    for axis, dim in sides:
        count = lax.axis_size(axis)
        ends = count - 1
        head = lax.slice_in_dim(cells, 0, width, axis=dim)
        tail = lax.slice_in_dim(cells, cells.shape[dim] - width, cells.shape[dim], axis=dim)
        cells = jnp.concatenate(
            [
                lax.ppermute(tail, axis, [(i, (i + 1) % count) for i in range(ends)]),
                cells,
                lax.ppermute(head, axis, [((i + 1) % count, i) for i in range(ends)]),
            ],
            axis=dim,
        )
    return cells


def attend_block(query_tile, keyset, valueset, live_tiles):
    scores = jnp.einsum(
        "qhd,khd->hqk", query_tile, keyset, preferred_element_type=jnp.float32
    ) * HD ** (-0.5)
    live = jnp.arange(keyset.shape[0], dtype=jnp.int32) // TILE < live_tiles
    masked = jnp.where(live[None, None, :], scores, -jnp.inf)
    row_top = jnp.max(masked, axis=2, keepdims=True)
    weights_raw = jnp.where(live[None, None, :], jnp.exp(masked - row_top), 0.0)
    denominator = jnp.sum(weights_raw, axis=2, keepdims=True)
    weights = (weights_raw / denominator).astype(jnp.bfloat16)
    blended = jnp.einsum("hqk,khd->qhd", weights, valueset, preferred_element_type=jnp.float32)
    return blended.astype(jnp.bfloat16)


def attend_tiles(query_rows, key_rows, value_rows, tile_lists, counts):
    tile_count = tile_lists.shape[0]
    head_count = query_rows.shape[1]
    query_tiles = query_rows.reshape(tile_count, TILE, head_count, HD)
    key_tiles = key_rows.reshape(3 * tile_count, TILE, head_count, HD)
    value_tiles = value_rows.reshape(3 * tile_count, TILE, head_count, HD)

    def one_tile(inputs):
        query_tile, listed, live_tiles = inputs
        keyset = key_tiles[listed].reshape(-1, head_count, HD)
        valueset = value_tiles[listed].reshape(-1, head_count, HD)
        return attend_block(query_tile, keyset, valueset, live_tiles)

    blended = lax.map(one_tile, (query_tiles, tile_lists, counts))
    return blended.reshape(tile_count * TILE, head_count, HD)


def body(queries, keys, values, neighbours, counts):
    shard_rows = queries.shape[0]
    head_groups = lax.axis_size("head")
    local_heads = queries.shape[1] // (head_groups * HD)
    slab_rows = shard_rows * head_groups
    stacked = jnp.stack((queries, keys, values)).reshape(
        3, shard_rows, head_groups, local_heads, HD
    )
    first_tile = (lax.axis_index("slab") - 1) * neighbours.shape[0]
    tile_lists = neighbours - first_tile
    exchanged = lax.all_to_all(stacked, "head", split_axis=2, concat_axis=1, tiled=True)
    kv_rows = extended(exchanged[1:3], (("slab", 1),), slab_rows)
    blended = attend_tiles(
        exchanged[0][:, 0], kv_rows[0][:, 0], kv_rows[1][:, 0], tile_lists, counts
    )
    result = lax.all_to_all(
        blended.reshape(slab_rows, 1, local_heads, HD),
        "head",
        split_axis=0,
        concat_axis=1,
        tiled=True,
    )
    return result.reshape(shard_rows, -1)


def solution(mesh):
    placed = (
        P(("slab", "head"), None),
        P(("slab", "head"), None),
        P(("slab", "head"), None),
        P("slab", None),
        P("slab"),
    )
    return jax.shard_map(
        body, mesh=mesh, in_specs=placed, out_specs=P(("slab", "head"), None), check_vma=False
    )
```

profile of v0, /device:TPU:23, one launch (start us, length us, event | category | flops | bytes accessed | tf_op | source)
XLA Modules:
  0.0 764.5 jit_solution(2532050491437162817)
XLA Ops:
  9.5 10.6 %pad_maximum_fusion.1 = bf16[3,192,16,2,128]{4,3,2,1,0:T(2,128)(2,1)} fusion(bf16[1,192,16,2,128]{4,3,2,1,0:T(2,128)(2,1)} %stack.14, bf16[1,192,16,2,128]{4,3,2,1,0:T(2,128)(2,1)S(1)} %stack.13, bf16[1,192,16,2,128]{4,3,2,1,0:T(2,128)(2,1)S(1)} %stack.12), kind=kLoop, calls=%fused_computation.36 | loop fusion | flops 4718592 | bytes 9437184 | tf_op jit(solution)/shard_map/stack | solution.py:63
  20.1 9.7 %copy.32 = bf16[3,192,16,2,128]{4,3,1,0,2:T(2,128)(2,1)} copy(bf16[3,192,16,2,128]{4,3,2,1,0:T(2,128)(2,1)} %pad_maximum_fusion.1) | data formatting | bytes 9437184 | tf_op jit(solution)/shard_map/stack | solution.py:63
  29.7 59.2 %all_to_all.30 = bf16[3,192,16,2,128]{4,3,1,0,2:T(2,128)(2,1)S(1)} all-to-all(bf16[3,192,16,2,128]{4,3,1,0,2:T(2,128)(2,1)} %copy.32), channel_id=1, replica_groups=mesh['slab'=8,'head'=16] {'head'}, dimensions={2} | all-to-all | bytes 9437184 | tf_op jit(solution)/shard_map/all_to_all | solution.py:68
  102.8 128.4 %collective-permute-done = bf16[2,3072,1,2,128]{4,1,3,0,2:T(8,128)(2,1)} collective-permute-done((bf16[2,3072,1,2,128]{4,1,3,0,2:T(8,128)(2,1)S(1)}, bf16[2,3072,1,2,128]{4,1,3,0,2:T(8,128)(2,1)}, u32[]{:S(2)}, u32[]{:S(2)}) %collective-permute-start) | collective-permute-done | bytes 3145760 | tf_op jit(solution)/shard_map/ppermute | solution.py:18
  234.3 12.3 %pad_maximum_fusion = bf16[2,9216,1,2,128]{4,1,3,0,2:T(8,128)(2,1)S(1)} fusion(bf16[2,3072,1,2,128]{4,1,3,0,2:T(8,128)(2,1)} %collective-permute-done.1, bf16[2,3072,1,2,128]{4,1,3,0,2:T(8,128)(2,1)S(1)} %bitcast.57, bf16[2,3072,1,2,128]{4,1,3,0,2:T(8,128)(2,1)} %collective-permute-done), kind=kLoop, calls=%fused_computation.35 | loop fusion | flops 28311552 | bytes 18874368 | tf_op jit(solution)/shard_map/concatenate | solution.py:16
  260.9 9.4 %copy.36 = bf16[24,384,2,128]{3,2,1,0:T(2,128)(2,1)} copy(bf16[24,384,2,128]{3,1,0,2:T(8,128)(2,1)} %bitcast.53) | data formatting | bytes 9437184 | tf_op jit(solution)/shard_map/while | solution.py:54
  270.3 461.0 %while.12 = (s32[]{:T(128)}, bf16[8,384,2,128]{3,1,0,2:T(8,128)(2,1)}, s32[8,12]{1,0:T(8,128)S(1)}, bf16[24,384,2,128]{3,2,1,0:T(2,128)(2,1)}, s32[8]{0:T(128)S(...) while((s32[]{:T(128)}, bf16[8,384,2,128]{3,1,0,2:T(8,128)(2,1)}, ...), condition=%wide.region_3.4_spmd, body=%wide.region_0.3_spmd.sunk | while | flops 1836857344 | bytes 71979352 | solution.py:54
  270.5 9.5 %gather_fusion = bf16[12,384,2,128]{3,2,1,0:T(2,128)(2,1)S(1)} fusion(bf16[24,384,2,128]{3,2,1,0:T(2,128)(2,1)} %get-tuple-element.211, s32[1024]{0:T(1024)S(1)} %pad_clamp_fusion.2), kind=kCustom, calls=%fused_computation.1.clone.1 | custom fusion | bytes 4718640 | tf_op jit(solution)/shard_map/while/body/eval_jaxpr/gather | solution.py:50
  289.3 20.9 %fusion.42 = (f32[2,384]{1,0:T(2,128)S(1)}, f32[2,384,4608]{2,1,0:T(8,128)}) fusion(f32[2,384,4608]{2,1,0:T(8,128)} %fusion.40, pred[4608]{0:T(1024)(128)(4,1)S(1)} %fusion.41), kind=kOutput, calls=%fused_computation.39.clone.1 | output fusion | flops 17699328 | bytes 28319232 | tf_op jit(solution)/shard_map/while/body/eval_jaxpr/sub | solution.py:34
  310.2 9.5 %gather_fusion.1 = bf16[12,384,2,128]{3,2,1,0:T(2,128)(2,1)S(1)} fusion(bf16[24,384,2,128]{3,2,1,0:T(2,128)(2,1)} %get-tuple-element.208, s32[1024]{0:T(1024)S(1)} %pad_clamp_fusion.2), kind=kCustom, calls=%fused_computation.clone.1 | custom fusion | bytes 4718640 | tf_op jit(solution)/shard_map/while/body/eval_jaxpr/gather | solution.py:51
  328.1 9.5 %gather_fusion = bf16[12,384,2,128]{3,2,1,0:T(2,128)(2,1)S(1)} fusion(bf16[24,384,2,128]{3,2,1,0:T(2,128)(2,1)} %get-tuple-element.211, s32[1024]{0:T(1024)S(1)} %pad_clamp_fusion.2), kind=kCustom, calls=%fused_computation.1.clone.1 | custom fusion | bytes 4718640 | tf_op jit(solution)/shard_map/while/body/eval_jaxpr/gather | solution.py:50
  346.9 20.9 %fusion.42 = (f32[2,384]{1,0:T(2,128)S(1)}, f32[2,384,4608]{2,1,0:T(8,128)}) fusion(f32[2,384,4608]{2,1,0:T(8,128)} %fusion.40, pred[4608]{0:T(1024)(128)(4,1)S(1)} %fusion.41), kind=kOutput, calls=%fused_computation.39.clone.1 | output fusion | flops 17699328 | bytes 28319232 | tf_op jit(solution)/shard_map/while/body/eval_jaxpr/sub | solution.py:34
  367.8 9.5 %gather_fusion.1 = bf16[12,384,2,128]{3,2,1,0:T(2,128)(2,1)S(1)} fusion(bf16[24,384,2,128]{3,2,1,0:T(2,128)(2,1)} %get-tuple-element.208, s32[1024]{0:T(1024)S(1)} %pad_clamp_fusion.2), kind=kCustom, calls=%fused_computation.clone.1 | custom fusion | bytes 4718640 | tf_op jit(solution)/shard_map/while/body/eval_jaxpr/gather | solution.py:51
  385.7 9.5 %gather_fusion = bf16[12,384,2,128]{3,2,1,0:T(2,128)(2,1)S(1)} fusion(bf16[24,384,2,128]{3,2,1,0:T(2,128)(2,1)} %get-tuple-element.211, s32[1024]{0:T(1024)S(1)} %pad_clamp_fusion.2), kind=kCustom, calls=%fused_computation.1.clone.1 | custom fusion | bytes 4718640 | tf_op jit(solution)/shard_map/while/body/eval_jaxpr/gather | solution.py:50
  404.4 20.9 %fusion.42 = (f32[2,384]{1,0:T(2,128)S(1)}, f32[2,384,4608]{2,1,0:T(8,128)}) fusion(f32[2,384,4608]{2,1,0:T(8,128)} %fusion.40, pred[4608]{0:T(1024)(128)(4,1)S(1)} %fusion.41), kind=kOutput, calls=%fused_computation.39.clone.1 | output fusion | flops 17699328 | bytes 28319232 | tf_op jit(solution)/shard_map/while/body/eval_jaxpr/sub | solution.py:34
  425.4 9.5 %gather_fusion.1 = bf16[12,384,2,128]{3,2,1,0:T(2,128)(2,1)S(1)} fusion(bf16[24,384,2,128]{3,2,1,0:T(2,128)(2,1)} %get-tuple-element.208, s32[1024]{0:T(1024)S(1)} %pad_clamp_fusion.2), kind=kCustom, calls=%fused_computation.clone.1 | custom fusion | bytes 4718640 | tf_op jit(solution)/shard_map/while/body/eval_jaxpr/gather | solution.py:51
  443.2 9.5 %gather_fusion = bf16[12,384,2,128]{3,2,1,0:T(2,128)(2,1)S(1)} fusion(bf16[24,384,2,128]{3,2,1,0:T(2,128)(2,1)} %get-tuple-element.211, s32[1024]{0:T(1024)S(1)} %pad_clamp_fusion.2), kind=kCustom, calls=%fused_computation.1.clone.1 | custom fusion | bytes 4718640 | tf_op jit(solution)/shard_map/while/body/eval_jaxpr/gather | solution.py:50
  462.0 20.9 %fusion.42 = (f32[2,384]{1,0:T(2,128)S(1)}, f32[2,384,4608]{2,1,0:T(8,128)}) fusion(f32[2,384,4608]{2,1,0:T(8,128)} %fusion.40, pred[4608]{0:T(1024)(128)(4,1)S(1)} %fusion.41), kind=kOutput, calls=%fused_computation.39.clone.1 | output fusion | flops 17699328 | bytes 28319232 | tf_op jit(solution)/shard_map/while/body/eval_jaxpr/sub | solution.py:34
  482.9 9.5 %gather_fusion.1 = bf16[12,384,2,128]{3,2,1,0:T(2,128)(2,1)S(1)} fusion(bf16[24,384,2,128]{3,2,1,0:T(2,128)(2,1)} %get-tuple-element.208, s32[1024]{0:T(1024)S(1)} %pad_clamp_fusion.2), kind=kCustom, calls=%fused_computation.clone.1 | custom fusion | bytes 4718640 | tf_op jit(solution)/shard_map/while/body/eval_jaxpr/gather | solution.py:51
  500.8 9.5 %gather_fusion = bf16[12,384,2,128]{3,2,1,0:T(2,128)(2,1)S(1)} fusion(bf16[24,384,2,128]{3,2,1,0:T(2,128)(2,1)} %get-tuple-element.211, s32[1024]{0:T(1024)S(1)} %pad_clamp_fusion.2), kind=kCustom, calls=%fused_computation.1.clone.1 | custom fusion | bytes 4718640 | tf_op jit(solution)/shard_map/while/body/eval_jaxpr/gather | solution.py:50
  519.6 20.9 %fusion.42 = (f32[2,384]{1,0:T(2,128)S(1)}, f32[2,384,4608]{2,1,0:T(8,128)}) fusion(f32[2,384,4608]{2,1,0:T(8,128)} %fusion.40, pred[4608]{0:T(1024)(128)(4,1)S(1)} %fusion.41), kind=kOutput, calls=%fused_computation.39.clone.1 | output fusion | flops 17699328 | bytes 28319232 | tf_op jit(solution)/shard_map/while/body/eval_jaxpr/sub | solution.py:34
  540.5 9.5 %gather_fusion.1 = bf16[12,384,2,128]{3,2,1,0:T(2,128)(2,1)S(1)} fusion(bf16[24,384,2,128]{3,2,1,0:T(2,128)(2,1)} %get-tuple-element.208, s32[1024]{0:T(1024)S(1)} %pad_clamp_fusion.2), kind=kCustom, calls=%fused_computation.clone.1 | custom fusion | bytes 4718640 | tf_op jit(solution)/shard_map/while/body/eval_jaxpr/gather | solution.py:51
  558.4 9.5 %gather_fusion = bf16[12,384,2,128]{3,2,1,0:T(2,128)(2,1)S(1)} fusion(bf16[24,384,2,128]{3,2,1,0:T(2,128)(2,1)} %get-tuple-element.211, s32[1024]{0:T(1024)S(1)} %pad_clamp_fusion.2), kind=kCustom, calls=%fused_computation.1.clone.1 | custom fusion | bytes 4718640 | tf_op jit(solution)/shard_map/while/body/eval_jaxpr/gather | solution.py:50
  577.2 20.9 %fusion.42 = (f32[2,384]{1,0:T(2,128)S(1)}, f32[2,384,4608]{2,1,0:T(8,128)}) fusion(f32[2,384,4608]{2,1,0:T(8,128)} %fusion.40, pred[4608]{0:T(1024)(128)(4,1)S(1)} %fusion.41), kind=kOutput, calls=%fused_computation.39.clone.1 | output fusion | flops 17699328 | bytes 28319232 | tf_op jit(solution)/shard_map/while/body/eval_jaxpr/sub | solution.py:34
  598.1 9.5 %gather_fusion.1 = bf16[12,384,2,128]{3,2,1,0:T(2,128)(2,1)S(1)} fusion(bf16[24,384,2,128]{3,2,1,0:T(2,128)(2,1)} %get-tuple-element.208, s32[1024]{0:T(1024)S(1)} %pad_clamp_fusion.2), kind=kCustom, calls=%fused_computation.clone.1 | custom fusion | bytes 4718640 | tf_op jit(solution)/shard_map/while/body/eval_jaxpr/gather | solution.py:51
  616.0 9.5 %gather_fusion = bf16[12,384,2,128]{3,2,1,0:T(2,128)(2,1)S(1)} fusion(bf16[24,384,2,128]{3,2,1,0:T(2,128)(2,1)} %get-tuple-element.211, s32[1024]{0:T(1024)S(1)} %pad_clamp_fusion.2), kind=kCustom, calls=%fused_computation.1.clone.1 | custom fusion | bytes 4718640 | tf_op jit(solution)/shard_map/while/body/eval_jaxpr/gather | solution.py:50
  634.8 20.9 %fusion.42 = (f32[2,384]{1,0:T(2,128)S(1)}, f32[2,384,4608]{2,1,0:T(8,128)}) fusion(f32[2,384,4608]{2,1,0:T(8,128)} %fusion.40, pred[4608]{0:T(1024)(128)(4,1)S(1)} %fusion.41), kind=kOutput, calls=%fused_computation.39.clone.1 | output fusion | flops 17699328 | bytes 28319232 | tf_op jit(solution)/shard_map/while/body/eval_jaxpr/sub | solution.py:34
  655.7 9.5 %gather_fusion.1 = bf16[12,384,2,128]{3,2,1,0:T(2,128)(2,1)S(1)} fusion(bf16[24,384,2,128]{3,2,1,0:T(2,128)(2,1)} %get-tuple-element.208, s32[1024]{0:T(1024)S(1)} %pad_clamp_fusion.2), kind=kCustom, calls=%fused_computation.clone.1 | custom fusion | bytes 4718640 | tf_op jit(solution)/shard_map/while/body/eval_jaxpr/gather | solution.py:51
  673.6 9.5 %gather_fusion = bf16[12,384,2,128]{3,2,1,0:T(2,128)(2,1)S(1)} fusion(bf16[24,384,2,128]{3,2,1,0:T(2,128)(2,1)} %get-tuple-element.211, s32[1024]{0:T(1024)S(1)} %pad_clamp_fusion.2), kind=kCustom, calls=%fused_computation.1.clone.1 | custom fusion | bytes 4718640 | tf_op jit(solution)/shard_map/while/body/eval_jaxpr/gather | solution.py:50
  692.4 20.9 %fusion.42 = (f32[2,384]{1,0:T(2,128)S(1)}, f32[2,384,4608]{2,1,0:T(8,128)}) fusion(f32[2,384,4608]{2,1,0:T(8,128)} %fusion.40, pred[4608]{0:T(1024)(128)(4,1)S(1)} %fusion.41), kind=kOutput, calls=%fused_computation.39.clone.1 | output fusion | flops 17699328 | bytes 28319232 | tf_op jit(solution)/shard_map/while/body/eval_jaxpr/sub | solution.py:34
  713.3 9.5 %gather_fusion.1 = bf16[12,384,2,128]{3,2,1,0:T(2,128)(2,1)S(1)} fusion(bf16[24,384,2,128]{3,2,1,0:T(2,128)(2,1)} %get-tuple-element.208, s32[1024]{0:T(1024)S(1)} %pad_clamp_fusion.2), kind=kCustom, calls=%fused_computation.clone.1 | custom fusion | bytes 4718640 | tf_op jit(solution)/shard_map/while/body/eval_jaxpr/gather | solution.py:51
  735.2 24.9 %all_to_all.31 = bf16[3072,1,2,128]{3,2,1,0:T(2,128)(2,1)S(1)} all-to-all(bf16[3072,1,2,128]{3,2,1,0:T(2,128)(2,1)S(1)} %copy.38), channel_id=1, replica_groups=mesh['slab'=8,'head'=16] {'head'}, dimensions={0} | all-to-all | bytes 3145728 | tf_op jit(solution)/shard_map/all_to_all | solution.py:73
  (87 shorter events, 189.6 us)
Async XLA Ops:
  90.1 2.1 copy-start
  90.1 10.0 %copy-start.1 = (s32[8,12]{1,0:T(8,128)S(1)}, s32[8,12]{1,0:T(8,128)}, u32[]{:S(2)}) copy-start(s32[8,12]{1,0:T(8,128)} %param.10) | copy-start | bytes 1156
  92.4 138.8 %collective-permute-start = (bf16[2,3072,1,2,128]{4,1,3,0,2:T(8,128)(2,1)S(1)}, bf16[2,3072,1,2,128]{4,1,3,0,2:T(8,128)(2,1)}, u32[]{:S(2)}, u32[]{:S(2)}) collective-permute-start(bf16[2,3072,1,2,128]{4,1,3,0,2:T(8,128)(2,1)S(1)} %bitcast.55), channel_id=1, source_target_pairs={{0,16},{16,32},{32,48},{48,64},{64,80},{80,96},{96,112},{1,17},{17... | collective-permute-start | bytes 9437192 | tf_op jit(solution)/shard_map/ppermute | solution.py:18
  97.7 136.6 %collective-permute-start.1 = (bf16[2,3072,1,2,128]{4,1,3,0,2:T(8,128)(2,1)S(1)}, bf16[2,3072,1,2,128]{4,1,3,0,2:T(8,128)(2,1)}, u32[]{:S(2)}, u32[]{:S(2)}) collective-permute-start(bf16[2,3072,1,2,128]{4,1,3,0,2:T(8,128)(2,1)S(1)} %bitcast.56), channel_id=1, source_target_pairs={{16,0},{32,16},{48,32},{64,48},{80,64},{96,80},{112,96},{17,1},{33... | collective-permute-start | bytes 9437192 | tf_op jit(solution)/shard_map/ppermute | solution.py:20
  260.9 9.4 %copy-start.2 = (s32[8]{0:T(128)S(1)}, s32[8]{0:T(128)}, u32[]{:S(2)}) copy-start(s32[8]{0:T(128)} %param.11) | copy-start | bytes 100
where the time goes:
time: 776 us; the launch traced here: 765 us
  local copies, waits for them, and re-layouts  221 us (28%)
  other arithmetic  196 us (25%)
  waiting for transfers between devices  131 us (17%)
  matrix products  124 us (16%)
  blocking collectives  84 us (11%)
    sub x8, other arithmetic, attend_block(): weights_raw = jnp.where(live[None, None, :], jnp.exp(masked - row_top), 0.0)  167 us
    ppermute x1, waiting for transfers between devices, extended(): lax.ppermute(tail, axis, [(i, (i + 1) % count) for i in range(ends)])  128 us
    gather x8, local copies, waits for them, and re-layouts, one_tile(): keyset = key_tiles[listed].reshape(-1, head_count, HD)  76 us
    gather x8, local copies, waits for them, and re-layouts, one_tile(): valueset = value_tiles[listed].reshape(-1, head_count, HD)  76 us
    dot_general x8, matrix products, attend_block(): jnp.einsum('qhd,khd->hqk', query_tile, keyset, preferred_element_type=jnp...  64 us
    dot_general x8, matrix products, attend_block(): jnp.einsum('hqk,khd->qhd', weights, valueset, preferred_element_type=jnp....  59.6 us
    all_to_all x1, blocking collectives, body(): lax.all_to_all(stacked, 'head', split_axis=2, concat_axis=1, tiled=True)  59.2 us
    all_to_all x1, blocking collectives, body(): lax.all_to_all(blended.reshape(slab_rows, 1, local_heads, HD), 'head', sp...  24.9 us
  transfers between devices with their start and end apart: 2, of which 2 were waited for; matrix products, arithmetic and copies ran while one was open for 0% of the time, Pallas kernels for 0%

commit v1 on v0

v1 whole, which is shorter than its diff:
```python
import functools
import math

import jax
import jax.numpy as jnp
from jax import lax
from jax.experimental import pallas as pl
from jax.experimental.pallas import tpu as pltpu
from jax.sharding import PartitionSpec as P

HD = 128
TILE = 384
HALF = TILE // 2
NB = 12
MESH = pl.DeviceIdType.MESH
SCALE = math.log2(math.e) / math.sqrt(HD)


def kernel(
    q_in, k_in, v_in, ints_in, out,
    kv0, kv1, q, o, s_buf, ints_v, ints_s,
    kv_recv, q_recv, send, fwd_recv, fwd_send, o_send, o_recv, int_recv, int_send, smem_sem,
):
    kv = (kv0, kv1)
    slab = lax.axis_index("slab")
    head = lax.axis_index("head")
    y, zh = slab // 2, slab % 2
    x, zl, core = head // 4, (head // 2) % 2, head % 2
    z = zh * 2 + zl
    frame = 2 * y + core
    pair = x * 4 + z

    def worker(wx, wz, wy, wcore):
        return (wy * 2 + wz // 2, (wx * 2 + wz % 2) * 2 + wcore)

    def is_me(where):
        return (where[0] == slab) & (where[1] == head)

    def step_dest(k):
        dx = k % 4
        dz = (k // 4 + dx) % 4
        return (x + dx) % 4, (z + dz) % 4

    up_y, up_core = (frame + 1) // 2, (frame + 1) % 2
    down_y, down_core = (frame + 1) // 2 - 1, (frame + 1) % 2
    up_dev = worker(x, z, up_y, up_core)
    down_dev = worker(x, z, down_y, down_core)
    has_up = frame < 7
    has_down = frame > 0

    barrier = pltpu.get_barrier_semaphore()

    def greet(k, count):
        wx, wz = step_dest(k)
        dest = worker(wx, wz, y, zh)
        source = (y * 2 + core, k)

        @pl.when(jnp.logical_not(is_me(dest)))
        def _():
            pl.semaphore_signal(barrier, inc=1, device_id=dest, device_id_type=MESH)

        @pl.when(jnp.logical_not(is_me(source)))
        def _():
            pl.semaphore_signal(barrier, inc=1, device_id=source, device_id_type=MESH)

        return count

    lax.fori_loop(0, 16, greet, 0)

    @pl.when(has_up)
    def _():
        pl.semaphore_signal(barrier, inc=1, device_id=up_dev, device_id_type=MESH)

    @pl.when(has_down)
    def _():
        pl.semaphore_signal(barrier, inc=1, device_id=down_dev, device_id_type=MESH)

    own = jnp.where(zh == core, 2, 0)
    pl.semaphore_wait(barrier, 32 - own + has_up.astype(jnp.int32) + has_down.astype(jnp.int32))

    partner = worker(x, core * 2 + zl, y, zh)

    @pl.when(zh == core)
    def _():
        pltpu.make_async_copy(ints_in, ints_v, int_recv).start()

    @pl.when(zh != core)
    def _():
        pltpu.make_async_remote_copy(
            ints_in, ints_v, int_send, int_recv, device_id=partner, device_id_type=MESH
        ).start()

    my_tile, my_row = head // 2, pl.multiple_of(core * HALF, HALF)

    def exchange(h, k, which):
        wx, wz = step_dest(k)
        dest = worker(wx, wz, y, zh)
        col = pl.multiple_of((wx * 4 + wz) * 256 + h * 128, 128)
        src_of = (q_in, k_in, v_in)
        for a in which:
            src = src_of[a].at[:, pl.ds(col, 128)]
            if a == 0:
                dst = q.at[h, my_tile, pl.ds(my_row, HALF), :]
                sem = q_recv.at[h]
            else:
                dst = kv[h].at[a - 1, 8 + my_tile, pl.ds(my_row, HALF), :]
                sem = kv_recv.at[h, head]

            @pl.when(is_me(dest))
            def _():
                pltpu.make_async_copy(src, dst, sem).start()

            @pl.when(jnp.logical_not(is_me(dest)))
            def _():
                pltpu.make_async_remote_copy(
                    src, dst, send.at[h, k], sem, device_id=dest, device_id_type=MESH
                ).start()

    def send_all(h, which):
        def body(k, carry):
            exchange(h, k, which)
            return carry

        lax.fori_loop(0, 16, body, 0)

    for h in range(2):
        send_all(h, (1, 2))
        send_all(h, (0,))

    def forward(h, k):
        dx = k % 4
        dz = (k // 4 + dx) % 4
        sx, sz = (x + 4 - dx) % 4, (z + 4 - dz) % 4

        @pl.when(sz // 2 == core)
        def _():
            for c in range(2):
                tile = sx * 2 + sz % 2
                src = kv[h].at[:, 8 + tile, pl.ds(c * HALF, HALF), :]
                pltpu.make_async_copy(src, src, kv_recv.at[h, tile * 2 + c]).wait()

                @pl.when(has_up)
                def _():
                    pltpu.make_async_remote_copy(
                        src, kv[h].at[:, tile, pl.ds(c * HALF, HALF), :],
                        fwd_send.at[h, 0], fwd_recv.at[h, 0], device_id=up_dev, device_id_type=MESH,
                    ).start()

                @pl.when(has_down)
                def _():
                    pltpu.make_async_remote_copy(
                        src, kv[h].at[:, 16 + tile, pl.ds(c * HALF, HALF), :],
                        fwd_send.at[h, 1], fwd_recv.at[h, 1], device_id=down_dev, device_id_type=MESH,
                    ).start()

    def forward_body(k, carry):
        forward(0, k)
        return carry

    lax.fori_loop(0, 16, forward_body, 0)

    pltpu.make_async_copy(ints_v, ints_v, int_recv).wait()
    to_smem = pltpu.make_async_copy(ints_v, ints_s, smem_sem)
    to_smem.start()
    to_smem.wait()

    def arrived(h):
        pltpu.make_async_copy(q.at[h], q.at[h], q_recv.at[h]).wait()

        @pl.when(has_down)
        def _():
            part = kv[h].at[:, pl.ds(0, 8)]
            pltpu.make_async_copy(part, part, fwd_recv.at[h, 0]).wait()

        @pl.when(has_up)
        def _():
            part = kv[h].at[:, pl.ds(16, 8)]
            pltpu.make_async_copy(part, part, fwd_recv.at[h, 1]).wait()

    def attend(h, a):
        qf = q[h, a].astype(jnp.float32) * SCALE
        hi = qf.astype(jnp.bfloat16)
        lo = (qf - hi.astype(jnp.float32)).astype(jnp.bfloat16)
        q2 = jnp.concatenate([hi, lo], axis=1)
        base = 8 * (frame - 1)
        index = [jnp.clip(ints_s[a, s] - base, 0, 23) for s in range(NB)]
        count = ints_s[a, NB]
        top = None
        for p in range(NB // 2):
            keys = jnp.concatenate([kv[h][0, index[2 * p]], kv[h][0, index[2 * p + 1]]], axis=0)
            keys2 = jnp.concatenate([keys, keys], axis=1)
            s = lax.dot_general(q2, keys2, (((1,), (1,)), ((), ())), preferred_element_type=jnp.float32)
            s_buf[p] = s
            m = s[:, 0:128]
            for c in range(1, 6):
                m = jnp.maximum(m, s[:, c * 128:(c + 1) * 128])
            top = m if top is None else jnp.maximum(top, m)
        row_top = jnp.max(top, axis=1, keepdims=True)
        acc = jnp.zeros((TILE, 256), jnp.float32)
        for p in range(NB // 2):
            w = jnp.exp2(s_buf[p] - row_top).astype(jnp.bfloat16)
            vals = []
            for s in (2 * p, 2 * p + 1):
                v = kv[h][1, index[s]]
                one = jnp.ones((TILE, 128), jnp.bfloat16)
                if s >= 6:
                    live = s < count
                    v = jnp.where(live, v, jnp.zeros_like(v))
                    one = jnp.where(live, one, jnp.zeros_like(one))
                vals.append(jnp.concatenate([v, one], axis=1))
            acc += jnp.dot(w, jnp.concatenate(vals, axis=0), preferred_element_type=jnp.float32)
        o[h, a] = (acc[:, :128] / acc[:, 128:]).astype(jnp.bfloat16)

    def o_target(a, half):
        return (y * 2 + core, 2 * a + half)

    def o_copy(h, a, half):
        col = pl.multiple_of((pair * 2 + h) * 128, 128)
        src = o.at[h, a, pl.ds(half * HALF, HALF), :]
        return src, out.at[:, pl.ds(col, 128)]

    def item(h, a, carry):
        i = h * 8 + a
        if h == 0:
            forward(1, 2 * a)
            forward(1, 2 * a + 1)
        attend(h, a)
        for half in range(2):
            dest = o_target(a, half)
            src, dst = o_copy(h, a, half)

            @pl.when(is_me(dest))
            def _():
                pltpu.make_async_copy(src, dst, o_recv).start()

            @pl.when(jnp.logical_not(is_me(dest)))
            def _():
                pltpu.make_async_remote_copy(
                    src, dst, o_send.at[i * 2 + half], o_recv, device_id=dest, device_id_type=MESH
                ).start()

        return carry

    for h in range(2):
        arrived(h)
        lax.fori_loop(0, 8, functools.partial(item, h), 0)

    def finish(k, carry):
        wx, wz = step_dest(k)

        @pl.when(jnp.logical_not(is_me(worker(wx, wz, y, zh))))
        def _():
            for h in range(2):
                part = q.at[h, pl.ds(0, 3), pl.ds(0, HALF), :]
                pltpu.make_async_copy(part, part, send.at[h, k]).wait()

        for half in range(2):
            a = k % 8

            @pl.when(jnp.logical_not(is_me(o_target(a, half))))
            def _():
                part = o.at[0, 0, pl.ds(0, HALF), :]
                pltpu.make_async_copy(part, part, o_send.at[k * 2 + half]).wait()

        return carry

    lax.fori_loop(0, 16, finish, 0)
    for h in range(2):
        part = kv[h].at[:, pl.ds(0, 8)]

        @pl.when(has_up)
        def _():
            pltpu.make_async_copy(part, part, fwd_send.at[h, 0]).wait()

        @pl.when(has_down)
        def _():
            pltpu.make_async_copy(part, part, fwd_send.at[h, 1]).wait()

    @pl.when(zh != core)
    def _():
        pltpu.make_async_copy(ints_v, ints_v, int_send).wait()

    pltpu.make_async_copy(out, out, o_recv).wait()


def body(queries, keys, values, neighbours, counts):
    ints = jnp.pad(jnp.concatenate([neighbours, counts[:, None]], axis=1), ((0, 0), (0, 128 - NB - 1)))
    any_space = pl.BlockSpec(memory_space=pl.ANY)
    dma = pltpu.SemaphoreType.DMA
    return pl.pallas_call(
        kernel,
        out_shape=jax.ShapeDtypeStruct(queries.shape, queries.dtype),
        in_specs=[any_space] * 4,
        out_specs=any_space,
        scratch_shapes=[
            pltpu.VMEM((2, 24, TILE, HD), jnp.bfloat16),
            pltpu.VMEM((2, 24, TILE, HD), jnp.bfloat16),
            pltpu.VMEM((2, 8, TILE, HD), jnp.bfloat16),
            pltpu.VMEM((2, 8, TILE, HD), jnp.bfloat16),
            pltpu.VMEM((NB // 2, TILE, 2 * TILE), jnp.float32),
            pltpu.VMEM((8, 128), jnp.int32),
            pltpu.SMEM((8, 128), jnp.int32),
            dma((2, 16)),
            dma((2,)),
            dma((2, 16)),
            dma((2, 2)),
            dma((2, 2)),
            dma((32,)),
            dma,
            dma,
            dma,
            dma,
        ],
        compiler_params=pltpu.CompilerParams(
            collective_id=0, has_side_effects=True, vmem_limit_bytes=56 * 1024 * 1024
        ),
    )(queries, keys, values, ints)


def solution(mesh):
    placed = (
        P(("slab", "head"), None),
        P(("slab", "head"), None),
        P(("slab", "head"), None),
        P("slab", None),
        P("slab"),
    )
    return jax.shard_map(
        body, mesh=mesh, in_specs=placed, out_specs=P(("slab", "head"), None), check_vma=False
    )
```

time: 776 us -> 118 us (0.15)
  the two profiles are of different devices: /device:TPU:23 before, /device:TPU:47 now
where the time goes in v1:
time: 118 us
  Pallas kernels  113 us (96%)
  local copies, waits for them, and re-layouts  4.03 us (3%)
    pallas_call x1, Pallas kernels, body(): pl.pallas_call(kernel, out_shape=jax.ShapeDtypeStruct(queries.shape, quer...  113 us
    unnamed x1, local copies, waits for them, and re-layouts  2.7 us

profile of v1, /device:TPU:47, one launch (start us, length us, event | category | flops | bytes accessed | tf_op | source)
XLA Modules:
  0.0 117.9 jit_solution(8612049850705864525)
XLA Ops:
  0.0 0.7 copy.6
  0.7 0.8 pad_add_fusion
  1.5 0.6 pad.4.ints_in
  2.1 113.1 %shard_map.55 = bf16[192,4096]{1,0:T(8,128)(2,1)} custom-call(bf16[192,4096]{1,0:T(8,128)(2,1)} %q_in.1, bf16[192,4096]{1,0:T(8,128)(2,1)} %k_in.1, bf16[192,4096]{1,0:T(8,128)(2,1)} %v_in.1, s32[8,128]{1,0:T(8,128)} %pad.4.ints_in), custom_call_target="tpu_custom_call" | custom-call | tf_op jit(solution)/shard_map/pallas_call | solution.py:290
  115.2 2.7 %copy.8 = bf16[192,4096]{1,0:T(8,128)(2,1)} copy(bf16[192,4096]{1,0:T(8,128)(2,1)} %shard_map.55) | data formatting | bytes 3145728

commit v2 on v1

--- a/solution.py
+++ b/solution.py
@@ -18,7 +18,7 @@
 
 def kernel(
     q_in, k_in, v_in, ints_in, out,
-    kv0, kv1, q, o, s_buf, ints_v, ints_s,
+    kv0, kv1, q, o, s_even, s_odd, top_even, top_odd, ints_v, ints_s,
     kv_recv, q_recv, send, fwd_recv, fwd_send, o_send, o_recv, int_recv, int_send, smem_sem,
 ):
     kv = (kv0, kv1)
@@ -177,39 +177,50 @@
             part = kv[h].at[:, pl.ds(16, 8)]
             pltpu.make_async_copy(part, part, fwd_recv.at[h, 1]).wait()
 
-    def attend(h, a):
-        qf = q[h, a].astype(jnp.float32) * SCALE
-        hi = qf.astype(jnp.bfloat16)
-        lo = (qf - hi.astype(jnp.float32)).astype(jnp.bfloat16)
-        q2 = jnp.concatenate([hi, lo], axis=1)
-        base = 8 * (frame - 1)
-        index = [jnp.clip(ints_s[a, s] - base, 0, 23) for s in range(NB)]
-        count = ints_s[a, NB]
-        top = None
+    base = 8 * (frame - 1)
+
+    def tiles_of(a):
+        return [jnp.clip(ints_s[a, s] - base, 0, 23) for s in range(NB)]
+
+    def score(h, a, p, index, s_ref, top):
+        keys = jnp.concatenate([kv[h][0, index[2 * p]], kv[h][0, index[2 * p + 1]]], axis=0)
+        s = lax.dot_general(q[h, a], keys, (((1,), (1,)), ((), ())), preferred_element_type=jnp.float32)
+        s_ref[p] = s
+        for c in range(6):
+            m = s[:, c * 128:(c + 1) * 128]
+            top = m if top is None else jnp.maximum(top, m)
+        return top
+
+    def keep_top(top, top_ref):
+        top_ref[...] = jnp.broadcast_to(jnp.max(top, axis=1, keepdims=True), (TILE, 128))
+
+    def blend(h, a, p, index, s_ref, row_top):
+        w = jnp.exp2((s_ref[p] - row_top) * SCALE).astype(jnp.bfloat16)
+        vals = []
+        for s in (2 * p, 2 * p + 1):
+            v = kv[h][1, index[s]]
+            one = jnp.ones((TILE, 128), jnp.bfloat16)
+            if s >= 6:
+                live = ints_s[a, s] != ints_s[a, 0]
+                v = jnp.where(live, v, jnp.zeros_like(v))
+                one = jnp.where(live, one, jnp.zeros_like(one))
+            vals.append(jnp.concatenate([v, one], axis=1))
+        return jnp.dot(w, jnp.concatenate(vals, axis=0), preferred_element_type=jnp.float32)
+
+    def attend(h, a, cur, nxt):
+        index = tiles_of(a)
+        row_top = cur[1][:, 0:1]
+        total, top = None, None
+        if nxt is not None:
+            index_next = tiles_of(a + 1)
         for p in range(NB // 2):
-            keys = jnp.concatenate([kv[h][0, index[2 * p]], kv[h][0, index[2 * p + 1]]], axis=0)
-            keys2 = jnp.concatenate([keys, keys], axis=1)
-            s = lax.dot_general(q2, keys2, (((1,), (1,)), ((), ())), preferred_element_type=jnp.float32)
-            s_buf[p] = s
-            m = s[:, 0:128]
-            for c in range(1, 6):
-                m = jnp.maximum(m, s[:, c * 128:(c + 1) * 128])
-            top = m if top is None else jnp.maximum(top, m)
-        row_top = jnp.max(top, axis=1, keepdims=True)
-        acc = jnp.zeros((TILE, 256), jnp.float32)
-        for p in range(NB // 2):
-            w = jnp.exp2(s_buf[p] - row_top).astype(jnp.bfloat16)
-            vals = []
-            for s in (2 * p, 2 * p + 1):
-                v = kv[h][1, index[s]]
-                one = jnp.ones((TILE, 128), jnp.bfloat16)
-                if s >= 6:
-                    live = s < count
-                    v = jnp.where(live, v, jnp.zeros_like(v))
-                    one = jnp.where(live, one, jnp.zeros_like(one))
-                vals.append(jnp.concatenate([v, one], axis=1))
-            acc += jnp.dot(w, jnp.concatenate(vals, axis=0), preferred_element_type=jnp.float32)
-        o[h, a] = (acc[:, :128] / acc[:, 128:]).astype(jnp.bfloat16)
+            if nxt is not None:
+                top = score(h, a + 1, p, index_next, nxt[0], top)
+            part = blend(h, a, p, index, cur[0], row_top)
+            total = part if total is None else total + part
+        if nxt is not None:
+            keep_top(top, nxt[1])
+        o[h, a] = (total[:, :128] / total[:, 128:]).astype(jnp.bfloat16)
 
     def o_target(a, half):
         return (y * 2 + core, 2 * a + half)
@@ -219,12 +230,14 @@
         src = o.at[h, a, pl.ds(half * HALF, HALF), :]
         return src, out.at[:, pl.ds(col, 128)]
 
-    def item(h, a, carry):
+    even, odd = (s_even, top_even), (s_odd, top_odd)
+
+    def item(h, a, cur, nxt):
         i = h * 8 + a
         if h == 0:
             forward(1, 2 * a)
             forward(1, 2 * a + 1)
-        attend(h, a)
+        attend(h, a, cur, nxt)
         for half in range(2):
             dest = o_target(a, half)
             src, dst = o_copy(h, a, half)
@@ -239,11 +252,21 @@
                     src, dst, o_send.at[i * 2 + half], o_recv, device_id=dest, device_id_type=MESH
                 ).start()
 
-        return carry
-
     for h in range(2):
         arrived(h)
-        lax.fori_loop(0, 8, functools.partial(item, h), 0)
+        first, top = tiles_of(0), None
+        for p in range(NB // 2):
+            top = score(h, 0, p, first, s_even, top)
+        keep_top(top, top_even)
+
+        def two(j, carry):
+            item(h, 2 * j, even, odd)
+            item(h, 2 * j + 1, odd, even)
+            return carry
+
+        lax.fori_loop(0, 3, two, 0)
+        item(h, 6, even, odd)
+        item(h, 7, odd, None)
 
     def finish(k, carry):
         wx, wz = step_dest(k)
@@ -284,7 +307,6 @@
 
 
 def body(queries, keys, values, neighbours, counts):
-    ints = jnp.pad(jnp.concatenate([neighbours, counts[:, None]], axis=1), ((0, 0), (0, 128 - NB - 1)))
     any_space = pl.BlockSpec(memory_space=pl.ANY)
     dma = pltpu.SemaphoreType.DMA
     return pl.pallas_call(
@@ -298,8 +320,11 @@
             pltpu.VMEM((2, 8, TILE, HD), jnp.bfloat16),
             pltpu.VMEM((2, 8, TILE, HD), jnp.bfloat16),
             pltpu.VMEM((NB // 2, TILE, 2 * TILE), jnp.float32),
-            pltpu.VMEM((8, 128), jnp.int32),
-            pltpu.SMEM((8, 128), jnp.int32),
+            pltpu.VMEM((NB // 2, TILE, 2 * TILE), jnp.float32),
+            pltpu.VMEM((TILE, 128), jnp.float32),
+            pltpu.VMEM((TILE, 128), jnp.float32),
+            pltpu.VMEM((8, NB), jnp.int32),
+            pltpu.SMEM((8, NB), jnp.int32),
             dma((2, 16)),
             dma((2,)),
             dma((2, 16)),
@@ -314,7 +339,7 @@
         compiler_params=pltpu.CompilerParams(
             collective_id=0, has_side_effects=True, vmem_limit_bytes=56 * 1024 * 1024
         ),
-    )(queries, keys, values, ints)
+    )(queries, keys, values, neighbours)
 
 
 def solution(mesh):

time: 118 us -> 96.5 us (0.82)
  the two profiles are of different devices: /device:TPU:47 before, /device:TPU:23 now
where the time goes in v2:
time: 96.5 us; the launch traced here: 96.4 us
  Pallas kernels  93.7 us (97%)
  local copies, waits for them, and re-layouts  2.7 us (3%)
    pallas_call x1, Pallas kernels, body(): pl.pallas_call(kernel, out_shape=jax.ShapeDtypeStruct(queries.shape, quer...  93.7 us
    unnamed x1, local copies, waits for them, and re-layouts  2.7 us

profile of v2, /device:TPU:23, one launch (start us, length us, event | category | flops | bytes accessed | tf_op | source)
XLA Modules:
  0.0 96.4 jit_solution(10842547683236138557)
XLA Ops:
  0.0 93.7 %shard_map.46 = bf16[192,4096]{1,0:T(8,128)(2,1)} custom-call(bf16[192,4096]{1,0:T(8,128)(2,1)} %q_in.1, bf16[192,4096]{1,0:T(8,128)(2,1)} %k_in.1, bf16[192,4096]{1,0:T(8,128)(2,1)} %v_in.1, s32[8,12]{1,0:T(8,128)} %ints_in.1), custom_call_target="tpu_custom_call" | custom-call | tf_op jit(solution)/shard_map/pallas_call | solution.py:312
  93.7 2.7 %copy.6 = bf16[192,4096]{1,0:T(8,128)(2,1)} copy(bf16[192,4096]{1,0:T(8,128)(2,1)} %shard_map.46) | data formatting | bytes 3145728

commit v3 on v2

--- a/solution.py
+++ b/solution.py
@@ -101,7 +101,7 @@
             src = src_of[a].at[:, pl.ds(col, 128)]
             if a == 0:
                 dst = q.at[h, my_tile, pl.ds(my_row, HALF), :]
-                sem = q_recv.at[h]
+                sem = q_recv.at[h, my_tile]
             else:
                 dst = kv[h].at[a - 1, 8 + my_tile, pl.ds(my_row, HALF), :]
                 sem = kv_recv.at[h, head]
@@ -153,20 +153,26 @@
                         fwd_send.at[h, 1], fwd_recv.at[h, 1], device_id=down_dev, device_id_type=MESH,
                     ).start()
 
-    def forward_body(k, carry):
-        forward(0, k)
+    def forward_body(h, k, carry):
+        forward(h, k)
         return carry
 
-    lax.fori_loop(0, 16, forward_body, 0)
+    lax.fori_loop(0, 16, functools.partial(forward_body, 0), 0)
 
     pltpu.make_async_copy(ints_v, ints_v, int_recv).wait()
     to_smem = pltpu.make_async_copy(ints_v, ints_s, smem_sem)
     to_smem.start()
     to_smem.wait()
 
+    def tile_at(n):
+        side = 1 - n % 2
+        dx = (z + 8 - n // 2 - 2 * core - side) % 4
+        return ((x + 4 - dx) % 4) * 2 + side
+
+    def query_arrived(h, a):
+        pltpu.make_async_copy(q.at[h, a], q.at[h, a], q_recv.at[h, a]).wait()
+
     def arrived(h):
-        pltpu.make_async_copy(q.at[h], q.at[h], q_recv.at[h]).wait()
-
         @pl.when(has_down)
         def _():
             part = kv[h].at[:, pl.ds(0, 8)]
@@ -207,15 +213,18 @@
             vals.append(jnp.concatenate([v, one], axis=1))
         return jnp.dot(w, jnp.concatenate(vals, axis=0), preferred_element_type=jnp.float32)
 
-    def attend(h, a, cur, nxt):
+    def attend(h, n, cur, nxt):
+        a = tile_at(n)
         index = tiles_of(a)
         row_top = cur[1][:, 0:1]
         total, top = None, None
         if nxt is not None:
-            index_next = tiles_of(a + 1)
+            after = tile_at(n + 1)
+            query_arrived(h, after)
+            index_next = tiles_of(after)
         for p in range(NB // 2):
             if nxt is not None:
-                top = score(h, a + 1, p, index_next, nxt[0], top)
+                top = score(h, after, p, index_next, nxt[0], top)
             part = blend(h, a, p, index, cur[0], row_top)
             total = part if total is None else total + part
         if nxt is not None:
@@ -232,12 +241,26 @@
 
     even, odd = (s_even, top_even), (s_odd, top_odd)
 
-    def item(h, a, cur, nxt):
-        i = h * 8 + a
+    def item(h, n, cur, nxt):
         if h == 0:
-            forward(1, 2 * a)
-            forward(1, 2 * a + 1)
-        attend(h, a, cur, nxt)
+
+            @pl.when(n >= 2)
+            def _():
+                forward(1, 2 * n - 4)
+                forward(1, 2 * n - 3)
+
+        if h == 1:
+
+            @pl.when(n < 4)
+            def _():
+                give(0, tile_at(2 * n))
+                give(0, tile_at(2 * n + 1))
+
+        attend(h, n, cur, nxt)
+        if h == 1:
+            give(1, tile_at(n))
+
+    def give(h, a):
         for half in range(2):
             dest = o_target(a, half)
             src, dst = o_copy(h, a, half)
@@ -249,14 +272,18 @@
             @pl.when(jnp.logical_not(is_me(dest)))
             def _():
                 pltpu.make_async_remote_copy(
-                    src, dst, o_send.at[i * 2 + half], o_recv, device_id=dest, device_id_type=MESH
+                    src, dst, o_send.at[h * 16 + a * 2 + half], o_recv, device_id=dest, device_id_type=MESH
                 ).start()
 
     for h in range(2):
+        if h == 1:
+            lax.fori_loop(12, 16, functools.partial(forward_body, 1), 0)
         arrived(h)
-        first, top = tiles_of(0), None
+        first, top = tile_at(0), None
+        query_arrived(h, first)
+        index_first = tiles_of(first)
         for p in range(NB // 2):
-            top = score(h, 0, p, first, s_even, top)
+            top = score(h, first, p, index_first, s_even, top)
         keep_top(top, top_even)
 
         def two(j, carry):
@@ -309,7 +336,7 @@
 def body(queries, keys, values, neighbours, counts):
     any_space = pl.BlockSpec(memory_space=pl.ANY)
     dma = pltpu.SemaphoreType.DMA
-    return pl.pallas_call(
+    return settle(pl.pallas_call(
         kernel,
         out_shape=jax.ShapeDtypeStruct(queries.shape, queries.dtype),
         in_specs=[any_space] * 4,
@@ -326,7 +353,7 @@
             pltpu.VMEM((8, NB), jnp.int32),
             pltpu.SMEM((8, NB), jnp.int32),
             dma((2, 16)),
-            dma((2,)),
+            dma((2, 8)),
             dma((2, 16)),
             dma((2, 2)),
             dma((2, 2)),
@@ -339,7 +366,34 @@
         compiler_params=pltpu.CompilerParams(
             collective_id=0, has_side_effects=True, vmem_limit_bytes=56 * 1024 * 1024
         ),
-    )(queries, keys, values, neighbours)
+    )(queries, keys, values, neighbours))
+
+
+def settle(result):
+    def copy(src, dst, held, into, outof):
+        reads = [
+            pltpu.make_async_copy(src.at[pl.ds(i * 48, 48)], held.at[pl.ds(i * 48, 48)], into.at[i]) for i in range(4)
+        ]
+        writes = [
+            pltpu.make_async_copy(held.at[pl.ds(i * 48, 48)], dst.at[pl.ds(i * 48, 48)], outof.at[i]) for i in range(4)
+        ]
+        for c in reads:
+            c.start()
+        for r, c in zip(reads, writes):
+            r.wait()
+            c.start()
+        for c in writes:
+            c.wait()
+
+    return pl.pallas_call(
+        copy,
+        out_shape=jax.ShapeDtypeStruct(result.shape, result.dtype),
+        in_specs=[pl.BlockSpec(memory_space=pl.ANY)],
+        out_specs=pl.BlockSpec(memory_space=pl.ANY),
+        scratch_shapes=[
+            pltpu.VMEM(result.shape, result.dtype), pltpu.SemaphoreType.DMA((4,)), pltpu.SemaphoreType.DMA((4,))
+        ],
+    )(result)
 
 
 def solution(mesh):

time: 96.5 us -> 92.6 us (0.960)
  the two profiles are of different devices: /device:TPU:23 before, /device:TPU:13 now
where the time goes in v3:
time: 92.6 us; the launch traced here: 92.5 us
  Pallas kernels  92.3 us (100%)
    pallas_call x1, Pallas kernels, body(): pl.pallas_call(kernel, out_shape=jax.ShapeDtypeStruct(queries.shape, quer...  90.1 us
    pallas_call x1, Pallas kernels, settle(): pl.pallas_call(copy, out_shape=jax.ShapeDtypeStruct(result.shape, result....  2.2 us

profile of v3, /device:TPU:13, one launch (start us, length us, event | category | flops | bytes accessed | tf_op | source)
XLA Modules:
  0.0 92.5 jit_solution(6752752673654699482)
XLA Ops:
  0.0 90.1 %shard_map.46.src = bf16[192,4096]{1,0:T(8,128)(2,1)} custom-call(bf16[192,4096]{1,0:T(8,128)(2,1)} %q_in.1, bf16[192,4096]{1,0:T(8,128)(2,1)} %k_in.1, bf16[192,4096]{1,0:T(8,128)(2,1)} %v_in.1, s32[8,12]{1,0:T(8,128)} %ints_in.1), custom_call_target="tpu_custom_call" | custom-call | tf_op jit(solution)/shard_map/pallas_call | solution.py:339
  90.1 2.2 %shard_map.47 = bf16[192,4096]{1,0:T(8,128)(2,1)} custom-call(bf16[192,4096]{1,0:T(8,128)(2,1)} %shard_map.46.src), custom_call_target="tpu_custom_call" | custom-call | tf_op jit(solution)/shard_map/pallas_call | solution.py:388

commit v4 on v3

--- a/solution.py
+++ b/solution.py
@@ -38,7 +38,7 @@
 
     def step_dest(k):
         dx = k % 4
-        dz = (k // 4 + dx) % 4
+        dz = (k // 4 + 4 - dx) % 4
         return (x + dx) % 4, (z + dz) % 4
 
     up_y, up_core = (frame + 1) // 2, (frame + 1) % 2
@@ -116,20 +116,22 @@
                     src, dst, send.at[h, k], sem, device_id=dest, device_id_type=MESH
                 ).start()
 
-    def send_all(h, which):
+    def send_all(h, which, first=0, last=16):
         def body(k, carry):
             exchange(h, k, which)
             return carry
 
-        lax.fori_loop(0, 16, body, 0)
-
-    for h in range(2):
-        send_all(h, (1, 2))
-        send_all(h, (0,))
+        lax.fori_loop(first, last, body, 0)
+
+    send_all(0, (1, 2))
+    send_all(0, (0,), 0, 12)
+    send_all(1, (1, 2))
+    send_all(0, (0,), 12, 16)
+    send_all(1, (0,))
 
     def forward(h, k):
         dx = k % 4
-        dz = (k // 4 + dx) % 4
+        dz = (k // 4 + 4 - dx) % 4
         sx, sz = (x + 4 - dx) % 4, (z + 4 - dz) % 4
 
         @pl.when(sz // 2 == core)
@@ -166,7 +168,7 @@
 
     def tile_at(n):
         side = 1 - n % 2
-        dx = (z + 8 - n // 2 - 2 * core - side) % 4
+        dx = (2 * core + side + n // 2 + 4 - z) % 4
         return ((x + 4 - dx) % 4) * 2 + side
 
     def query_arrived(h, a):
@@ -190,7 +192,13 @@
 
     def score(h, a, p, index, s_ref, top):
         keys = jnp.concatenate([kv[h][0, index[2 * p]], kv[h][0, index[2 * p + 1]]], axis=0)
-        s = lax.dot_general(q[h, a], keys, (((1,), (1,)), ((), ())), preferred_element_type=jnp.float32)
+        halves = [
+            lax.dot_general(
+                q[h, a, i * HALF:(i + 1) * HALF], keys, (((1,), (1,)), ((), ())), preferred_element_type=jnp.float32
+            )
+            for i in range(2)
+        ]
+        s = jnp.concatenate(halves, axis=0)
         s_ref[p] = s
         for c in range(6):
             m = s[:, c * 128:(c + 1) * 128]
@@ -244,10 +252,11 @@
     def item(h, n, cur, nxt):
         if h == 0:
 
-            @pl.when(n >= 2)
-            def _():
-                forward(1, 2 * n - 4)
-                forward(1, 2 * n - 3)
+            @pl.when((n >= 2) & (n <= 5))
+            def _():
+                start = jnp.where(n == 2, 0, 2 * n - 2)
+                stop = jnp.where(n == 5, 16, 2 * n)
+                lax.fori_loop(start, stop, functools.partial(forward_body, 1), 0)
 
         if h == 1:
 
@@ -276,8 +285,6 @@
                 ).start()
 
     for h in range(2):
-        if h == 1:
-            lax.fori_loop(12, 16, functools.partial(forward_body, 1), 0)
         arrived(h)
         first, top = tile_at(0), None
         query_arrived(h, first)

time: 92.6 us -> 90.9 us (0.982)
  the two profiles are of different devices: /device:TPU:13 before, /device:TPU:23 now
where the time goes in v4:
time: 90.9 us; the launch traced here: 89.4 us
  Pallas kernels  89.3 us (98%)
    pallas_call x1, Pallas kernels, body(): pl.pallas_call(kernel, out_shape=jax.ShapeDtypeStruct(queries.shape, quer...  87.1 us
    pallas_call x1, Pallas kernels, settle(): pl.pallas_call(copy, out_shape=jax.ShapeDtypeStruct(result.shape, result....  2.2 us

profile of v4, /device:TPU:23, one launch (start us, length us, event | category | flops | bytes accessed | tf_op | source)
XLA Modules:
  0.0 89.4 jit_solution(16764027126441706117)
XLA Ops:
  0.0 87.1 %shard_map.46.src = bf16[192,4096]{1,0:T(8,128)(2,1)} custom-call(bf16[192,4096]{1,0:T(8,128)(2,1)} %q_in.1, bf16[192,4096]{1,0:T(8,128)(2,1)} %k_in.1, bf16[192,4096]{1,0:T(8,128)(2,1)} %v_in.1, s32[8,12]{1,0:T(8,128)} %ints_in.1), custom_call_target="tpu_custom_call" | custom-call | tf_op jit(solution)/shard_map/pallas_call | solution.py:346
  87.1 2.2 %shard_map.47 = bf16[192,4096]{1,0:T(8,128)(2,1)} custom-call(bf16[192,4096]{1,0:T(8,128)(2,1)} %shard_map.46.src), custom_call_target="tpu_custom_call" | custom-call | tf_op jit(solution)/shard_map/pallas_call | solution.py:395

commit v5 on v4

--- a/solution.py
+++ b/solution.py
@@ -208,8 +208,8 @@
     def keep_top(top, top_ref):
         top_ref[...] = jnp.broadcast_to(jnp.max(top, axis=1, keepdims=True), (TILE, 128))
 
-    def blend(h, a, p, index, s_ref, row_top):
-        w = jnp.exp2((s_ref[p] - row_top) * SCALE).astype(jnp.bfloat16)
+    def blend(h, a, p, index, s_ref, row_top, rows=slice(None)):
+        w = jnp.exp2((s_ref[p, rows] - row_top) * SCALE).astype(jnp.bfloat16)
         vals = []
         for s in (2 * p, 2 * p + 1):
             v = kv[h][1, index[s]]
@@ -269,8 +269,8 @@
         if h == 1:
             give(1, tile_at(n))
 
-    def give(h, a):
-        for half in range(2):
+    def give(h, a, halves=(0, 1)):
+        for half in halves:
             dest = o_target(a, half)
             src, dst = o_copy(h, a, half)
 
@@ -300,7 +300,19 @@
 
         lax.fori_loop(0, 3, two, 0)
         item(h, 6, even, odd)
-        item(h, 7, odd, None)
+        if h == 0:
+            item(h, 7, odd, None)
+
+    last = tile_at(7)
+    index_last = tiles_of(last)
+    for half in range(2):
+        rows = slice(half * HALF, (half + 1) * HALF)
+        total = None
+        for p in range(NB // 2):
+            part = blend(1, last, p, index_last, s_odd, top_odd[rows, 0:1], rows)
+            total = part if total is None else total + part
+        o[1, last, rows] = (total[:, :128] / total[:, 128:]).astype(jnp.bfloat16)
+        give(1, last, (half,))
 
     def finish(k, carry):
         wx, wz = step_dest(k)

time: 90.9 us -> 90.9 us (level)
  no operation moved by 1% of the time
where the time goes in v5:
time: 90.9 us; the launch traced here: 89.2 us
  Pallas kernels  89.1 us (98%)
    pallas_call x1, Pallas kernels, body(): pl.pallas_call(kernel, out_shape=jax.ShapeDtypeStruct(queries.shape, quer...  86.9 us
    pallas_call x1, Pallas kernels, settle(): pl.pallas_call(copy, out_shape=jax.ShapeDtypeStruct(result.shape, result....  2.2 us

profile of v5, /device:TPU:23, one launch (start us, length us, event | category | flops | bytes accessed | tf_op | source)
XLA Modules:
  0.0 89.2 jit_solution(1316725750558548998)
XLA Ops:
  0.0 86.9 %shard_map.46.src = bf16[192,4096]{1,0:T(8,128)(2,1)} custom-call(bf16[192,4096]{1,0:T(8,128)(2,1)} %q_in.1, bf16[192,4096]{1,0:T(8,128)(2,1)} %k_in.1, bf16[192,4096]{1,0:T(8,128)(2,1)} %v_in.1, s32[8,12]{1,0:T(8,128)} %ints_in.1), custom_call_target="tpu_custom_call" | custom-call | tf_op jit(solution)/shard_map/pallas_call | solution.py:358
  86.9 2.2 %shard_map.47 = bf16[192,4096]{1,0:T(8,128)(2,1)} custom-call(bf16[192,4096]{1,0:T(8,128)(2,1)} %shard_map.46.src), custom_call_target="tpu_custom_call" | custom-call | tf_op jit(solution)/shard_map/pallas_call | solution.py:407

commit v6 on v5

--- a/solution.py
+++ b/solution.py
@@ -260,10 +260,10 @@
 
         if h == 1:
 
-            @pl.when(n < 4)
-            def _():
-                give(0, tile_at(2 * n))
-                give(0, tile_at(2 * n + 1))
+            @pl.when(n < 2)
+            def _():
+                for j in range(4):
+                    give(0, tile_at(4 * n + j))
 
         attend(h, n, cur, nxt)
         if h == 1:

time: 90.9 us -> 90.9 us (level)
  no operation moved by 1% of the time
where the time goes in v6:
time: 90.9 us; the launch traced here: 89.2 us
  Pallas kernels  89.1 us (98%)
    pallas_call x1, Pallas kernels, body(): pl.pallas_call(kernel, out_shape=jax.ShapeDtypeStruct(queries.shape, quer...  86.9 us
    pallas_call x1, Pallas kernels, settle(): pl.pallas_call(copy, out_shape=jax.ShapeDtypeStruct(result.shape, result....  2.2 us

profile of v6, /device:TPU:23, one launch (start us, length us, event | category | flops | bytes accessed | tf_op | source)
XLA Modules:
  0.0 89.2 jit_solution(4292297212419004316)
XLA Ops:
  0.0 86.9 %shard_map.46.src = bf16[192,4096]{1,0:T(8,128)(2,1)} custom-call(bf16[192,4096]{1,0:T(8,128)(2,1)} %q_in.1, bf16[192,4096]{1,0:T(8,128)(2,1)} %k_in.1, bf16[192,4096]{1,0:T(8,128)(2,1)} %v_in.1, s32[8,12]{1,0:T(8,128)} %ints_in.1), custom_call_target="tpu_custom_call" | custom-call | tf_op jit(solution)/shard_map/pallas_call | solution.py:358
  86.9 2.2 %shard_map.47 = bf16[192,4096]{1,0:T(8,128)(2,1)} custom-call(bf16[192,4096]{1,0:T(8,128)(2,1)} %shard_map.46.src), custom_call_target="tpu_custom_call" | custom-call | tf_op jit(solution)/shard_map/pallas_call | solution.py:407
